TPU v7x, 32 devices: a whole 2x2x4 slice. The times are simulated.
32 devices in a mesh: dp: 16 (over z, y, core), slab: 2 (over x).
Axes of the slice: x: 2, y: 2, z: 4, core: 2. Of those that a mesh axis runs over, the one named last changes fastest.
Arguments:
- snapshots: bfloat16 [16, 64, 512, 512], P('dp', None, 'slab'), may hold values from -6 to 6
- cotangent: bfloat16 [16, 64, 512, 512], P('dp', None, 'slab'), may hold values from -6 to 6
- w_spec: float32 [32, 32, 64, 128], P('slab', 'dp'), may hold values from -0.5 to 0.5
- first_moment: float32 [32, 32, 64, 128], P('slab', 'dp'), may hold values from -6 to 6
- second_moment: float32 [32, 32, 64, 128], P('slab', 'dp'), may hold values from 0.1 to 4
- w_skip: bfloat16 [64, 64], replicated, may hold values from -0.75 to 0.75
- bias: float32 [64], replicated, may hold values from -3 to 3
Outputs:
- layer_out: bfloat16 [16, 64, 512, 512], P('dp', None, 'slab')
- new_weights: float32 [32, 32, 64, 128], P('slab', 'dp')
- new_first: float32 [32, 32, 64, 128], P('slab', 'dp')
- new_second: float32 [32, 32, 64, 128], P('slab', 'dp')
All inputs are finite; a program needn't handle non-finite values.
Results may differ from a plain program's by a relative error of at most 0.001.
Values sent between devices are 32-bit elements; how exact they have to be, the bound alone decides.
A program may use at most 192 MiB of HBM per device.

v0:
```python
import math

import jax
import jax.numpy as jnp
from jax import lax
from jax.sharding import PartitionSpec as P

NY = 512
NZ = 512
KY = 32
KZ = 32


high = lax.Precision.HIGHEST
gelu_coef = 0.7978845608028654
cube_coef = 0.044715


def gelu_value(x):
    return 0.5 * x * (1.0 + jnp.tanh(gelu_coef * (x + cube_coef * x * x * x)))


def gelu_slope(x):
    tanh_val = jnp.tanh(gelu_coef * (x + cube_coef * x * x * x))
    return 0.5 * (1.0 + tanh_val) + 0.5 * x * (1.0 - tanh_val * tanh_val) * gelu_coef * (
        1.0 + 3.0 * cube_coef * x * x
    )


def z_tables(length):
    zpos = jnp.arange(length, dtype=jnp.int32)[:, None]
    kpos = jnp.arange(KZ, dtype=jnp.int32)[None, :]
    angle = 2.0 * math.pi / length * jnp.remainder(zpos * kpos, length).astype(jnp.float32)
    return (jnp.cos(angle), jnp.sin(angle))


def y_tables(count):
    half = KY // 2
    freq = jnp.concatenate(
        [jnp.arange(half, dtype=jnp.int32), jnp.arange(half, dtype=jnp.int32) - half]
    )
    ypos = jnp.arange(count, dtype=jnp.int32)
    phase = jnp.remainder(ypos[:, None] * freq[None, :], NY)
    angle = 2.0 * math.pi / NY * phase.astype(jnp.float32)
    return (jnp.cos(angle), jnp.sin(angle))


def y_forward(flat, ycos, ysin, count):
    with_cos = jnp.einsum("cyk,yj->ckj", flat, ycos, precision=high)
    with_sin = jnp.einsum("cyk,yj->ckj", flat, ysin, precision=high)
    real_part = with_cos[:, :count] + with_sin[:, count:]
    imag_part = with_cos[:, count:] - with_sin[:, :count]
    return jnp.stack([real_part, imag_part], 0).transpose(2, 0, 1, 3)


def y_inverse(spec, ycos, ysin):
    vreal = spec[:, 0]
    vimag = spec[:, 1]
    yreal = jnp.einsum("koj,yj->oyk", vreal, ycos, precision=high) - jnp.einsum(
        "koj,yj->oyk", vimag, ysin, precision=high
    )
    yimag = jnp.einsum("koj,yj->oyk", vreal, ysin, precision=high) + jnp.einsum(
        "koj,yj->oyk", vimag, ycos, precision=high
    )
    return (yreal, yimag)


def forward_modes(field):
    chans, rows, length = field.shape
    zcos, zsin = z_tables(length)
    table = jnp.concatenate([zcos, -zsin], axis=1)
    along_z = jnp.dot(
        field.reshape(chans * rows, length),
        table,
        precision=high,
        preferred_element_type=jnp.float32,
    )
    along_z = along_z.reshape(chans, rows, 2, KZ)
    pencil = lax.all_to_all(along_z, "slab", split_axis=3, concat_axis=1, tiled=True)
    local_modes = pencil.shape[3]
    ycos, ysin = y_tables(NY)
    return y_forward(pencil.reshape(chans, NY, 2 * local_modes), ycos, ysin, local_modes)


def inverse_modes(spec, rows, length):
    chans = spec.shape[2]
    zcos, zsin = z_tables(length)
    ycos, ysin = y_tables(NY)
    yreal, yimag = y_inverse(spec, ycos, ysin)
    both = jnp.stack([yreal, yimag], 2)
    slabs = lax.all_to_all(both, "slab", split_axis=1, concat_axis=3, tiled=True)
    back_table = jnp.concatenate([zcos.T, -zsin.T], axis=0)
    total = jnp.dot(
        slabs.reshape(chans * rows, 2 * KZ),
        back_table,
        precision=high,
        preferred_element_type=jnp.float32,
    )
    return total.reshape(chans, rows, length)


def body(snapshots, cotangent, w_spec, first_moment, second_moment, w_skip, bias):
    chans, rows, length = snapshots.shape[1:]
    spec_scale = 1.0 / math.sqrt(NY * NZ)
    out_scale = 1.0 / math.sqrt(KY * KZ)
    count = lax.axis_size("dp")
    field_low = snapshots[0]
    weights = lax.all_gather(w_spec, "dp", axis=1, tiled=True)
    spec_u = forward_modes(field_low.astype(jnp.float32)) * spec_scale
    ureal = spec_u[:, 0]
    uimag = spec_u[:, 1]
    first_part = jnp.einsum("kij,kjio->koj", ureal, weights, precision=high)
    second_part = jnp.einsum("kij,kjio->koj", uimag, weights, precision=high)
    vreal = first_part[:, :chans] - second_part[:, chans:]
    vimag = first_part[:, chans:] + second_part[:, :chans]
    spec_v = jnp.stack([vreal, vimag], 1)
    mixed = inverse_modes(spec_v, rows, length) * out_scale
    skip = jnp.einsum(
        "io,in->on",
        w_skip,
        field_low.reshape(chans, rows * length),
        preferred_element_type=jnp.float32,
    )
    pre = mixed + skip.reshape(chans, rows, length) + bias[:, None, None]
    layer_out = gelu_value(pre).astype(jnp.bfloat16)[None]
    slope = cotangent[0].astype(jnp.float32) * gelu_slope(pre)
    spec_g = forward_modes(slope) * out_scale
    greal = spec_g[:, 0]
    gimag = spec_g[:, 1]
    grad_real = jnp.einsum("kij,koj->kjio", ureal, greal, precision=high) + jnp.einsum(
        "kij,koj->kjio", uimag, gimag, precision=high
    )
    grad_imag = jnp.einsum("kij,koj->kjio", ureal, gimag, precision=high) - jnp.einsum(
        "kij,koj->kjio", uimag, greal, precision=high
    )
    summed = lax.psum_scatter(
        jnp.concatenate([grad_real, grad_imag], axis=-1), "dp", scatter_dimension=1, tiled=True
    )
    grad = summed / count
    new_first = 0.9 * first_moment + 0.1 * grad
    new_second = 0.95 * second_moment + 0.05 * grad * grad
    bias_first = 1.0 - 0.9**10
    bias_second = 1.0 - 0.95**10
    new_weights = w_spec - 0.01 * (new_first / bias_first) / (
        jnp.sqrt(new_second / bias_second) + 1e-08
    )
    return (layer_out, new_weights, new_first, new_second)


def solution(mesh):
    placed = (
        P("dp", None, "slab", None),
        P("dp", None, "slab", None),
        P("slab", "dp", None, None),
        P("slab", "dp", None, None),
        P("slab", "dp", None, None),
        P(),
        P(),
    )
    return jax.shard_map(
        body,
        mesh=mesh,
        in_specs=placed,
        out_specs=(
            P("dp", None, "slab", None),
            P("slab", "dp", None, None),
            P("slab", "dp", None, None),
            P("slab", "dp", None, None),
        ),
        check_vma=False,
    )
```

profile of v0, /device:TPU:1, one launch (start us, length us, event | category | flops | bytes accessed | tf_op | source)
XLA Modules:
  0.0 820.5 jit_solution(16519467777478254915)
XLA Ops:
  8.2 18.1 %fusion.120 = f32[64,16384]{1,0:T(8,128)S(1)} fusion(bf16[16384,512]{1,0:T(8,128)(2,1)} %bitcast.145, f32[512,32]{0,1:T(8,128)S(1)} %get-tuple-element.19, f32[512,32]{0,1:T(8,128)S(1)} %get-tuple-element.20), kind=kOutput, calls=%fused_computation.154 | convolution fusion | flops 6442483712 | bytes 21102592 | tf_op jit(solution)/shard_map/dot_general | solution.py:72
  29.9 5.6 all-to-all-start
  35.6 47.6 %all-to-all-done = f32[64,256,2,32]{1,0,2,3:T(8,128)} async-done(((f32[64,256,2,32]{1,0,2,3:T(8,128)}), f32[64,256,2,32]{1,0,2,3:T(8,128)}, u32[]{:S(2)}, u32[]{:S(2)}) %all-to-all-start) | async-done | bytes 4194336 | tf_op jit(solution)/shard_map/all_to_all | solution.py:79
  83.2 7.4 copy.68
  90.6 6.6 reshape.41
  97.2 6.1 fusion.52
  103.3 6.1 fusion.58
  110.4 29.2 %all-gather.2.cloned.1.call-done = f32[16,32,64,128]{3,2,1,0:T(8,128)} async-done(((f32[16,2,64,128]{3,2,1,0:T(8,128)}), f32[16,32,64,128]{3,2,1,0:T(8,128)}) %all-gather.2.cloned.1.call-update) | async-done | bytes 16777232 | tf_op jit(solution)/shard_map/all_gather | solution.py:108
  139.7 17.5 %fusion.121 = f32[16,32,1,128]{3,2,1,0:T(1,128)S(1)} fusion(f32[16,64,32,1]{1,3,2,0:T(1,128)S(1)} %copy.43, f32[16,32,64,128]{3,2,1,0:T(8,128)} %all-gather.2.cloned.1.call-done), kind=kOutput, calls=%fused_computation.156 | convolution fusion | flops 50331648 | bytes 17170432 | tf_op jit(solution)/shard_map/kij,kjio->koj/dot_general | solution.py:112
  157.2 15.1 %fusion.122 = f32[16,32,1,128]{3,2,1,0:T(1,128)S(1)} fusion(f32[16,64,32,1]{1,3,2,0:T(1,128)S(1)} %copy.45, f32[16,32,64,128]{3,2,1,0:T(8,128)S(1)} %copy-done.2), kind=kOutput, calls=%fused_computation.157 | convolution fusion | flops 50331648 | bytes 17170432 | tf_op jit(solution)/shard_map/kij,kjio->koj/dot_general | solution.py:113
  183.9 9.1 %copy.32 = f32[64,512,2,16]{0,3,2,1:T(8,128)} copy(f32[64,512,2,16]{1,0,3,2:T(8,128)} %pad_maximum_fusion.1) | data formatting | bytes 8388608 | tf_op jit(solution)/shard_map/stack | solution.py:90
  193.0 8.7 %reshape.57 = f32[2,1,524288]{2,1,0:T(1,128)} reshape(f32[512,2,16,64]{3,2,1,0:T(8,128)} %bitcast.147) | data formatting | bytes 8388608
  201.7 5.6 all-to-all-start.1
  207.7 35.3 %fusion.19 = f32[64,256,512]{2,0,1:T(8,128)} fusion(bf16[64,64]{1,0:T(8,128)(2,1)S(1)} %copy-done, bf16[8,8,256,512]{3,2,1,0:T(8,128)(2,1)} %bitcast.146), kind=kOutput, calls=%fused_computation.21 | convolution fusion | flops 1073741824 | bytes 50339840 | tf_op jit(solution)/shard_map/io,in->on/dot_general | solution.py:118
  242.9 11.7 %all-to-all-done.1 = f32[2,1,524288]{2,1,0:T(1,128)} async-done(((f32[2,1,524288]{2,1,0:T(1,128)}), f32[2,1,524288]{2,1,0:T(1,128)}, u32[]{:S(2)}, u32[]{:S(2)}) %all-to-all-start.1) | async-done | bytes 4194336 | tf_op jit(solution)/shard_map/all_to_all | solution.py:91
  255.1 16.5 %reduce = f32[2,524288]{1,0:T(2,128)} reduce(f32[2,1,524288]{2,1,0:T(1,128)} %all-to-all-done.1, f32[]{:T(128)} %broadcast.184), dimensions={1}, to_apply=%all_to_all.36.reduce_sub_computation | reduce | bytes 8388612 | tf_op jit(solution)/shard_map/all_to_all | solution.py:91
  271.7 10.1 %reshape.58 = f32[512,2,16,64]{3,2,1,0:T(8,128)} reshape(f32[2,524288]{1,0:T(2,128)} %reduce) | data formatting | bytes 8388608
  281.8 8.7 %copy.33 = f32[64,2,256,2,16]{2,4,1,3,0:T(8,128)} copy(f32[64,2,256,2,16]{0,4,3,2,1:T(8,128)} %bitcast.148) | data formatting | bytes 8388608 | tf_op jit(solution)/shard_map/all_to_all | solution.py:91
  290.5 56.3 %fusion.10 = f32[64,256,512]{2,1,0:T(8,128)} fusion(f32[64,256,512]{2,0,1:T(8,128)} %fusion.19, f32[64]{0:T(128)S(1)} %copy-done.6, f32[64,256,64]{1,2,0:T(8,128)} %bitcast.149, f32[32,512]{1,0:T(8,128)S(1)} %get-tuple-element.21, f32[32,512]{1,0:T(8,128)S(1)} %get-tuple-element.22), kind=kOutput, calls=%fused_computation.12 | convolution fusion | flops 6467649536 | bytes 71434496 | tf_op jit(solution)/shard_map/dot_general | solution.py:93
  346.8 57.3 %fusion.7 = f32[64,256,2,32]{1,3,2,0:T(8,128)S(1)} fusion(f32[2,32,512,1]{2,1,0,3:T(8,128)S(1)} %bitcast.162, f32[64,256,512]{2,1,0:T(8,128)} %fusion.10, bf16[1,64,256,512]{3,2,1,0:T(8,128)(2,1)} %param.8), kind=kOutput, calls=%fused_computation.9 | convolution fusion | flops 6601834496 | bytes 54657024 | tf_op jit(solution)/shard_map/dot_general | solution.py:72
  404.1 5.2 copy.38
  409.3 5.6 all-to-all-start.2
  415.4 45.8 %all-to-all-done.2 = f32[64,256,2,32]{1,2,0,3:T(2,128)} async-done(((f32[64,256,2,32]{1,2,0,3:T(2,128)}), f32[64,256,2,32]{1,2,0,3:T(2,128)}, u32[]{:S(2)}, u32[]{:S(2)}) %all-to-all-start.2) | async-done | bytes 4194336 | tf_op jit(solution)/shard_map/all_to_all | solution.py:79
  461.2 7.4 copy.67
  468.7 6.7 reshape.42
  475.3 6.1 fusion.48
  481.5 6.1 fusion.54
  488.4 11.3 %multiply_add_fusion.1 = (f32[16,32,64,64]{3,2,1,0:T(8,128)S(1)}, f32[16,32,64,64]{3,2,1,0:T(8,128)}) fusion(f32[16,32,64]{2,1,0:T(8,128)S(1)} %copy.42, f32[16,32,64]{2,1,0:T(8,128)S(1)} %copy.41, f32[16,32,64]{2,1,0:T(8,128)S(1)} %copy.40, f32[16,32,64]{2,1,0:T(8,128)S(1)} %copy.37), kind=kLoop, calls=%fused_computation.27 | loop fusion | flops 12582912 | bytes 17301504 | tf_op jit(solution)/shard_map/add | solution.py:130
  499.7 13.1 %pad_maximum_fusion = f32[16,32,64,128]{3,2,1,0:T(8,128)} fusion(f32[16,32,64,64]{3,2,1,0:T(8,128)} %get-tuple-element.12, f32[16,32,64,64]{3,2,1,0:T(8,128)S(1)} %get-tuple-element.11), kind=kLoop, calls=%fused_computation.24 | loop fusion | flops 4194304 | bytes 33554432 | tf_op jit(solution)/shard_map/concatenate | solution.py:137
  514.8 22.2 %fusion.28 = bf16[1,64,256,512]{3,2,1,0:T(8,128)(2,1)} fusion(f32[64,256,512]{2,1,0:T(8,128)} %fusion.10), kind=kLoop, calls=%fused_computation.33 | loop fusion | flops 75497472 | bytes 50331648 | tf_op jit(solution)/shard_map/broadcast_in_dim | solution.py:125
  537.0 273.1 %all-reduce.3.cloned.1.call-done = f32[16,32,64,128]{3,2,1,0:T(8,128)} async-done(((f32[16,32,64,128]{3,2,1,0:T(8,128)}), f32[16,32,64,128]{3,2,1,0:T(8,128)}) %all-reduce.3.cloned.1.call-update) | async-done | bytes 16777232
  810.1 3.3 divide_subtract_fusion
  (47 shorter events, 20.6 us)
Async XLA Ops:
  7.2 200.5 %copy-start = (bf16[64,64]{1,0:T(8,128)(2,1)S(1)}, bf16[64,64]{1,0:T(8,128)(2,1)}, u32[]{:S(2)}) copy-start(bf16[64,64]{1,0:T(8,128)(2,1)} %param.12) | copy-start | bytes 24580
  7.2 132.5 %all-gather.2.cloned.1.call-start = ((), (), s32[]{:S(2)}) async-start(), calls=%async_computation.3 | async-start | bytes 17825792 | tf_op jit(solution)/shard_map/all_gather | solution.py:108
  29.9 53.3 %all-to-all-start = ((f32[64,256,2,32]{1,0,2,3:T(8,128)}), f32[64,256,2,32]{1,0,2,3:T(8,128)}, u32[]{:S(2)}, u32[]{:S(2)}) async-start(f32[64,256,2,32]{1,0,2,3:T(8,128)} %copy.30), calls=%async_computation | async-start | bytes 8388608 | tf_op jit(solution)/shard_map/all_to_all | solution.py:79
  139.7 17.5 %copy-start.2 = (f32[16,32,64,128]{3,2,1,0:T(8,128)S(1)}, f32[16,32,64,128]{3,2,1,0:T(8,128)}, u32[]{:S(2)}) copy-start(f32[16,32,64,128]{3,2,1,0:T(8,128)} %all-gather.2.cloned.1.call-done) | copy-start | bytes 50331652
  201.7 52.9 %all-to-all-start.1 = ((f32[2,1,524288]{2,1,0:T(1,128)}), f32[2,1,524288]{2,1,0:T(1,128)}, u32[]{:S(2)}, u32[]{:S(2)}) async-start(f32[2,1,524288]{2,1,0:T(1,128)} %reshape.57), calls=%async_computation.1 | async-start | bytes 8388608 | tf_op jit(solution)/shard_map/all_to_all | solution.py:91
  255.1 35.4 %copy-start.6 = (f32[64]{0:T(128)S(1)}, f32[64]{0:T(128)}, u32[]{:S(2)}) copy-start(f32[64]{0:T(128)} %param.13) | copy-start | bytes 772
  409.3 51.9 %all-to-all-start.2 = ((f32[64,256,2,32]{1,2,0,3:T(2,128)}), f32[64,256,2,32]{1,2,0,3:T(2,128)}, u32[]{:S(2)}, u32[]{:S(2)}) async-start(f32[64,256,2,32]{1,2,0,3:T(2,128)} %copy.38), calls=%async_computation.2 | async-start | bytes 8388608 | tf_op jit(solution)/shard_map/all_to_all | solution.py:79
  414.9 395.2 %all-reduce.3.cloned.1.call-start = ((), (), s32[]{:S(2)}) async-start(), calls=%async_computation.4 | async-start | bytes 33554432
  512.8 0.7 copy-start.7
  514.1 299.4 %copy-start.1 = (bf16[64,64]{1,0:T(8,128)(2,1)S(1)}, bf16[64,64]{1,0:T(8,128)(2,1)}, u32[]{:S(2)}) copy-start(bf16[64,64]{1,0:T(8,128)(2,1)} %param.12) | copy-start | bytes 24580
  514.7 295.4 %copy-start.3 = (f32[16,2,64,128]{3,2,1,0:T(8,128)S(1)}, f32[16,2,64,128]{3,2,1,0:T(8,128)}, u32[]{:S(2)}) copy-start(f32[16,2,64,128]{3,2,1,0:T(8,128)} %param.9) | copy-start | bytes 3145732
  514.7 295.4 %copy-start.4 = (f32[16,2,64,128]{3,2,1,0:T(8,128)S(1)}, f32[16,2,64,128]{3,2,1,0:T(8,128)}, u32[]{:S(2)}) copy-start(f32[16,2,64,128]{3,2,1,0:T(8,128)} %param.10) | copy-start | bytes 3145732
  514.7 295.4 %copy-start.5 = (f32[16,2,64,128]{3,2,1,0:T(8,128)S(1)}, f32[16,2,64,128]{3,2,1,0:T(8,128)}, u32[]{:S(2)}) copy-start(f32[16,2,64,128]{3,2,1,0:T(8,128)} %param.11) | copy-start | bytes 3145732
Sparse Core Ops, SparseCore 0:
  10.2 129.4 all-gather.1
  513.0 297.0 all-reduce.2
where the time goes:
time: 828 us; the launch traced here: 821 us
  waiting for transfers between devices  408 us (49%)
  matrix products  233 us (28%)
  local copies, waits for them, and re-layouts  77.1 us (9%)
  other arithmetic  70.1 us (8%)
  starting transfers between devices  16.8 us (2%)
  between operations  15.2 us (2%)
    unnamed x3, waiting for transfers between devices  274 us
    all_to_all x2, waiting for transfers between devices, forward_modes(): lax.all_to_all(along_z, 'slab', split_axis=3, concat_axis=1, tiled=True)  93.4 us
    dot_general x2, matrix products, forward_modes(): jnp.dot(field.reshape(chans * rows, length), table, precision=high, prefe...  75.4 us
    dot_general x1, matrix products, inverse_modes(): jnp.dot(slabs.reshape(chans * rows, 2 * KZ), back_table, precision=high,...  56.3 us
    dot_general x1, matrix products, body(): jnp.einsum('io,in->on', w_skip, field_low.reshape(chans, rows * length),...  35.3 us
    all_gather x1, waiting for transfers between devices, body(): weights = lax.all_gather(w_spec, 'dp', axis=1, tiled=True)  29.2 us
    broadcast_in_dim x1, other arithmetic, body(): layer_out = gelu_value(pre).astype(jnp.bfloat16)[None]  22.2 us
    unnamed x20, local copies, waits for them, and re-layouts  21.4 us
  transfers between devices with their start and end apart: 5, of which 5 were waited for; matrix products, arithmetic and copies ran while one was open for 13% of the time, Pallas kernels for 0%

commit v1 on v0

v1 whole, which is shorter than its diff:
```python
import functools
import math

import jax
import jax.numpy as jnp
import ml_dtypes
import numpy as np
from jax import lax
from jax.experimental import pallas as pl
from jax.experimental.pallas import tpu as pltpu
from jax.sharding import PartitionSpec as P

NY = 512
NZ = 512
KY = 32
KZ = 32
ROWS = 16

high = lax.Precision.HIGHEST
gelu_coef = 0.7978845608028654
cube_coef = 0.044715
vmem_bytes = 56 * 1024 * 1024


def halves(table):
    top = table.astype(ml_dtypes.bfloat16)
    rest = (table - top.astype(np.float64)).astype(ml_dtypes.bfloat16)
    return top, rest


def z_table():
    angle = 2.0 * math.pi / NZ * (np.outer(np.arange(NZ), np.arange(KZ)) % NZ)
    return np.concatenate([np.cos(angle), -np.sin(angle)], 1)


def y_table():
    freq = np.concatenate([np.arange(KY // 2), np.arange(KY // 2) - KY // 2])
    angle = 2.0 * math.pi / NY * (np.outer(np.arange(NY), freq) % NY)
    return np.concatenate([np.cos(angle), np.sin(angle)], 1)


def split(x):
    top = x.astype(jnp.bfloat16)
    return top, (x - top.astype(jnp.float32)).astype(jnp.bfloat16)


def mm(a, b):
    return jnp.dot(a, b, preferred_element_type=jnp.float32)


def y_modes(zval, ytab):
    top, rest = split(zval)
    both = mm(ytab, top)
    w = both[: 2 * KY] + both[2 * KY :] + mm(ytab[: 2 * KY], rest)
    real = w[:KY, :KZ] + w[KY:, KZ:]
    imag = w[:KY, KZ:] - w[KY:, :KZ]
    return jnp.concatenate([real, imag], axis=1)


def forward_kernel(x_ref, zt_ref, yt_ref, o_ref):
    for c in range(x_ref.shape[0]):
        zval = mm(x_ref[c], zt_ref[...])
        o_ref[c] = y_modes(zval[:, : 2 * KZ] + zval[:, 2 * KZ :], yt_ref[...])


def point_kernel(
    x_ref, cot_ref, spec_ref, bias_ref, kron_ref, zt_ref, yt_ref, back_ref, yback_ref,
    out_ref, g_ref, left, zsum,
):
    step = pl.program_id(0)
    chans, rows = left.shape[:2]
    wide = 2 * KZ

    @pl.when(step == 0)
    def _():
        @pl.loop(0, chans)
        def _(o):
            v = spec_ref[o]
            turned = jnp.concatenate([-v[:, KZ:], v[:, :KZ]], axis=1)
            top, rest = split(jnp.concatenate([v, turned], axis=0))
            yval = mm(yback_ref[...], jnp.concatenate([top, rest, top], axis=0))
            ytop, yrest = split(yval)
            b = bias_ref[o]
            b0 = b.astype(jnp.bfloat16).astype(jnp.float32)
            b1 = (b - b0).astype(jnp.bfloat16).astype(jnp.float32)
            lane = lax.broadcasted_iota(jnp.int32, b.shape, 1)
            terms = jnp.where(lane == 0, b0, jnp.where(lane == 1, b1, b - b0 - b1))
            terms = jnp.broadcast_to(terms, (rows, wide)).astype(jnp.bfloat16)
            left[o] = jnp.concatenate([ytop, yrest, ytop, terms], axis=1)

    here = pl.ds(pl.multiple_of(step * ROWS, ROWS), ROWS)
    x = x_ref[...].reshape(chans * ROWS, NZ)
    part = chans // 2
    for m in range(2):
        own = slice(m * part, (m + 1) * part)
        pre = mm(kron_ref[m * part * ROWS : (m + 1) * part * ROWS, :], x)
        pre += mm(left[own, here, :].reshape(part * ROWS, 4 * wide), back_ref[...])
        sq = pre * pre
        t = jnp.tanh(pre * (gelu_coef + (gelu_coef * cube_coef) * sq))
        h = 0.5 + 0.5 * t
        value = pre * h
        out_ref[own] = value.astype(jnp.bfloat16).reshape(part, ROWS, NZ)
        grow = 2.0 * gelu_coef + (6.0 * gelu_coef * cube_coef) * sq
        cot = cot_ref[own].reshape(part * ROWS, NZ).astype(jnp.float32)
        slope = cot * (h + value * (0.5 - 0.5 * t) * grow)
        top, rest = split(slope)
        zval = mm(top, zt_ref[...])
        zval = zval[:, :wide] + zval[:, wide:] + mm(rest, zt_ref[:, :wide])
        zsum[own, here, :] = zval.reshape(part, ROWS, wide)

    @pl.when(step == pl.num_programs(0) - 1)
    def _():
        @pl.loop(0, chans)
        def _(o):
            g_ref[o] = y_modes(zsum[o], yt_ref[...])


def whole(shape):
    return pl.BlockSpec(shape, lambda i: (0,) * len(shape))


def forward_modes(field, zt, yt):
    chans, rows, length = field.shape
    per = 8
    return pl.pallas_call(
        forward_kernel,
        grid=(chans // per,),
        in_specs=[
            pl.BlockSpec((per, rows, length), lambda i: (i, 0, 0)),
            whole(zt.shape),
            whole(yt.shape),
        ],
        out_specs=pl.BlockSpec((per, KY, 2 * KZ), lambda i: (i, 0, 0)),
        out_shape=jax.ShapeDtypeStruct((chans, KY, 2 * KZ), jnp.float32),
        compiler_params=pltpu.CompilerParams(vmem_limit_bytes=vmem_bytes),
    )(field, zt, yt)


def point_part(field, cot, spec, bias, kron, zt, yt, back, yback):
    chans, rows, length = field.shape
    rowed = pl.BlockSpec((chans, ROWS, length), lambda i: (0, i, 0))
    return pl.pallas_call(
        point_kernel,
        grid=(rows // ROWS,),
        in_specs=[rowed, rowed]
        + [whole(a.shape) for a in (spec, bias, kron, zt, yt, back, yback)],
        out_specs=[rowed, whole((chans, KY, 2 * KZ))],
        out_shape=[
            jax.ShapeDtypeStruct(field.shape, jnp.bfloat16),
            jax.ShapeDtypeStruct((chans, KY, 2 * KZ), jnp.float32),
        ],
        scratch_shapes=[
            pltpu.VMEM((chans, rows, 8 * KZ), jnp.bfloat16),
            pltpu.VMEM((chans, rows, 2 * KZ), jnp.float32),
        ],
        compiler_params=pltpu.CompilerParams(vmem_limit_bytes=vmem_bytes),
    )(field, cot, spec, bias, kron, zt, yt, back, yback)


def to_owner(modes, dp, slab):
    chans = modes.shape[0]
    x = modes.reshape(chans, dp, KY // dp, 2, slab, KZ // slab)
    x = x.transpose(1, 4, 5, 2, 3, 0).reshape(dp * slab, -1, chans)
    x = lax.all_to_all(x, ("dp", "slab"), split_axis=0, concat_axis=0, tiled=True)
    x = x.reshape(dp, slab, KZ // slab, KY // dp, 2, chans).sum(1)
    return x.transpose(1, 2, 0, 3, 4)


def from_owner(spec, dp, slab):
    chans = spec.shape[-1]
    x = spec.transpose(2, 0, 1, 3, 4).reshape(dp, 1, -1, chans)
    x = jnp.broadcast_to(x, (dp, slab) + x.shape[2:]).reshape(dp * slab, -1, chans)
    x = lax.all_to_all(x, ("dp", "slab"), split_axis=0, concat_axis=0, tiled=True)
    x = x.reshape(dp, slab, KZ // slab, KY // dp, 2, chans)
    return x.transpose(5, 0, 3, 4, 1, 2).reshape(chans, KY, 2 * KZ)


def body(snapshots, cotangent, w_spec, first_moment, second_moment, w_skip, bias):
    chans, rows, length = snapshots.shape[1:]
    spec_scale = 1.0 / math.sqrt(NY * NZ)
    out_scale = 1.0 / math.sqrt(KY * KZ)
    dp = lax.axis_size("dp")
    slab = lax.axis_size("slab")
    start = lax.axis_index("slab") * rows
    ztop, zrest = halves(z_table())
    ytop, yrest = halves(y_table())
    zt = jnp.asarray(np.concatenate([ztop, zrest], 1))
    ones = np.zeros((2 * KZ, length), ml_dtypes.bfloat16)
    ones[:3] = 1
    back = jnp.asarray(np.concatenate([ztop.T, ztop.T, zrest.T, ones], 0))
    yt = jnp.asarray(np.concatenate([ytop, yrest], 1).T)
    yt = lax.dynamic_slice_in_dim(yt, start, rows, 1)
    yback = jnp.asarray(np.concatenate([ytop, ytop, yrest], 1))
    yback = lax.dynamic_slice_in_dim(yback, start, rows, 0)
    same = jnp.eye(ROWS, dtype=jnp.bfloat16)
    kron = w_skip.T[:, None, :, None] * same[None, :, None, :]
    kron = kron.reshape(chans * ROWS, chans * ROWS)
    bias_lanes = jnp.pad(
        jnp.broadcast_to(bias[:, None, None], (chans, 1, 3)), ((0, 0), (0, 0), (0, 2 * KZ - 3))
    )

    u = to_owner(forward_modes(snapshots[0], zt, yt), dp, slab) * spec_scale
    prod = jnp.einsum("kjbri,kjio->kjbro", u, w_spec, precision=high)
    vreal = prod[..., 0, :chans] - prod[..., 1, chans:]
    vimag = prod[..., 0, chans:] + prod[..., 1, :chans]
    spec = from_owner(jnp.stack([vreal, vimag], 3) * out_scale, dp, slab)
    layer_out, gmodes = point_part(
        snapshots[0], cotangent[0], spec, bias_lanes, kron, zt, yt, back, yback
    )
    g = to_owner(gmodes, dp, slab) * (out_scale / dp)
    turned = jnp.stack([g[..., 1, :], -g[..., 0, :]], 3)
    pair = jnp.concatenate([g, turned], -1)
    grad = jnp.einsum("kjbri,kjbro->kjio", u, pair, precision=high)
    new_first = 0.9 * first_moment + 0.1 * grad
    new_second = 0.95 * second_moment + 0.05 * grad * grad
    bias_first = 1.0 - 0.9**10
    bias_second = 1.0 - 0.95**10
    new_weights = w_spec - 0.01 * (new_first / bias_first) / (
        jnp.sqrt(new_second / bias_second) + 1e-08
    )
    return (layer_out[None], new_weights, new_first, new_second)


def solution(mesh):
    placed = (
        P("dp", None, "slab", None),
        P("dp", None, "slab", None),
        P("slab", "dp", None, None),
        P("slab", "dp", None, None),
        P("slab", "dp", None, None),
        P(),
        P(),
    )
    return jax.shard_map(
        body,
        mesh=mesh,
        in_specs=placed,
        out_specs=(
            P("dp", None, "slab", None),
            P("slab", "dp", None, None),
            P("slab", "dp", None, None),
            P("slab", "dp", None, None),
        ),
        check_vma=False,
    )
```

time: 828 us -> 235 us (0.28)
  waiting for transfers between devices: 408 us -> 14.9 us
  matrix products: 233 us -> 7.18 us
  Pallas kernels: 0 us -> 114 us
  other arithmetic: 70.1 us -> 14.2 us
  local copies, waits for them, and re-layouts: 77.1 us -> 52.1 us
  blocking collectives: 0 us -> 21.5 us
  between operations: 15.2 us -> 0.85 us
    unnamed x3 -> x0, waiting for transfers between devices: 274 us -> none
    dot_general x14 -> x2, matrix products: 233 us -> 7.18 us  [the longest x1 5.84 us: body(): grad = jnp.einsum('kjbri,kjbro->kjio', u, pair, precision=high)]
    pallas_call x0 -> x2, Pallas kernels: none -> 114 us  [the longest x1 89.9 us: point_part(): pl.pallas_call(point_kernel, grid=(rows // ROWS,), in_specs=[rowed, rowed...]
    all_to_all x3 -> x2, waiting for transfers between devices: 105 us -> 14.9 us  [the longest x1 14.9 us: to_owner(): lax.all_to_all(x, ('dp', 'slab'), split_axis=0, concat_axis=0, tiled=True)]
    mul x0 -> x1, local copies, waits for them, and re-layouts: none -> 29.8 us  [body(): kron = w_skip.T[:, None, :, None] * same[None, :, None, :]]
    all_gather x1 -> x0, waiting for transfers between devices: 29.2 us -> none  [body(): weights = lax.all_gather(w_spec, 'dp', axis=1, tiled=True)]
    all_to_all x4 -> x1, local copies, waits for them, and re-layouts: 24.1 us -> 0.51 us  [to_owner(): lax.all_to_all(x, ('dp', 'slab'), split_axis=0, concat_axis=0, tiled=True)]
    broadcast_in_dim x1 -> x0, other arithmetic: 22.2 us -> none  [body(): layer_out = gelu_value(pre).astype(jnp.bfloat16)[None]]
  transfers between devices with their start and end apart: 5 -> 2, of which waited for: 5 -> 1; matrix products, arithmetic and copies ran while one was open for 13% -> 16% of each run, Pallas kernels for 0% -> 0%
where the time goes in v1:
time: 235 us; the launch traced here: 234 us
  Pallas kernels  114 us (49%)
  local copies, waits for them, and re-layouts  52.1 us (22%)
  blocking collectives  21.5 us (9%)
  waiting for transfers between devices  14.9 us (6%)
  other arithmetic  14.2 us (6%)
  starting transfers between devices  9.9 us (4%)
  matrix products  7.18 us (3%)
    pallas_call x1, Pallas kernels, point_part(): pl.pallas_call(point_kernel, grid=(rows // ROWS,), in_specs=[rowed, rowed...  89.9 us
    mul x1, local copies, waits for them, and re-layouts, body(): kron = w_skip.T[:, None, :, None] * same[None, :, None, :]  29.8 us
    pallas_call x1, Pallas kernels, forward_modes(): pl.pallas_call(forward_kernel, grid=(chans // per,), in_specs=[pl.BlockSp...  23.7 us
    all_to_all x1, blocking collectives, to_owner(): lax.all_to_all(x, ('dp', 'slab'), split_axis=0, concat_axis=0, tiled=True)  21.5 us
    all_to_all x1, waiting for transfers between devices, to_owner(): lax.all_to_all(x, ('dp', 'slab'), split_axis=0, concat_axis=0, tiled=True)  14.9 us
    unnamed x14, local copies, waits for them, and re-layouts  7.25 us
    all_to_all x1, starting transfers between devices, to_owner(): lax.all_to_all(x, ('dp', 'slab'), split_axis=0, concat_axis=0, tiled=True)  7.09 us
    mul x1, other arithmetic, body(): kron = w_skip.T[:, None, :, None] * same[None, :, None, :]  6.11 us
  transfers between devices with their start and end apart: 2, of which 1 were waited for; matrix products, arithmetic and copies ran while one was open for 16% of the time, Pallas kernels for 0%

profile of v1, /device:TPU:1, one launch (start us, length us, event | category | flops | bytes accessed | tf_op | source)
XLA Modules:
  0.0 234.3 jit_solution(11953373678194559298)
XLA Ops:
  0.7 1.6 constant_dynamic-slice_fusion.1.yt_ref
  2.2 23.7 %shard_map.138 = f32[64,32,64]{2,1,0:T(8,128)} custom-call(bf16[64,256,512]{2,1,0:T(8,128)(2,1)} %bitcast.41, bf16[512,128]{1,0:T(8,128)(2,1)} %constant.43.clone.zt_ref, bf16[128,256]{1,0:T(8,128)(2,1)} %constant_dynamic-slice_fusion.1.yt_ref), custom_call_target="tpu_custom_call" | custom-call | tf_op jit(solution)/shard_map/pallas_call | solution.py:125
  25.9 1.8 copy.25
  27.7 1.8 copy.26
  29.5 2.7 %reshape.64 = f32[32,1,4096]{2,1,0:T(1,128)} reshape(f32[32,64,64]{2,1,0:T(8,128)} %bitcast.47) | data formatting | bytes 1048576
  32.2 7.1 %all-to-all-start = ((f32[32,1,4096]{2,1,0:T(1,128)}), f32[32,1,4096]{2,1,0:T(1,128)S(1)}, u32[]{:S(2)}, u32[]{:S(2)}) async-start(f32[32,1,4096]{2,1,0:T(1,128)} %reshape.64), calls=%async_computation | async-start | bytes 1048576 | tf_op jit(solution)/shard_map/all_to_all | solution.py:164
  39.5 0.6 pad.4.bias_ref
  40.2 14.9 %all-to-all-done = f32[32,1,4096]{2,1,0:T(1,128)S(1)} async-done(((f32[32,1,4096]{2,1,0:T(1,128)}), f32[32,1,4096]{2,1,0:T(1,128)S(1)}, u32[]{:S(2)}, u32[]{:S(2)}) %all-to-all-start) | async-done | bytes 524320 | tf_op jit(solution)/shard_map/all_to_all | solution.py:164
  55.1 0.5 broadcast.28
  55.6 1.8 reduce
  57.4 0.4 reshape.65
  57.8 1.0 reduce_sum.18
  58.9 1.3 fusion.1
  60.8 1.4 reshape.66
  62.2 2.8 %all-to-all-start.1 = ((f32[32,1,4096]{2,1,0:T(1,128)}), f32[32,1,4096]{2,1,0:T(1,128)S(1)}, u32[]{:S(2)}, u32[]{:S(2)}) async-start(f32[32,1,4096]{2,1,0:T(1,128)} %reshape.66), calls=%async_computation.1 | async-start | bytes 1048576 | tf_op jit(solution)/shard_map/all_to_all | solution.py:173
  65.1 6.1 %broadcast_multiply_fusion = bf16[64,16,64,16]{3,2,1,0:T(8,128)(2,1)} fusion(bf16[16,16]{1,0:T(8,128)(2,1)S(1)} %fusion.13, bf16[64,64]{1,0:T(8,128)(2,1)S(1)} %copy.30), kind=kLoop, calls=%fused_computation | loop fusion | flops 1048576 | bytes 2105856 | tf_op jit(solution)/shard_map/mul | solution.py:196
  71.2 29.8 %mul.79.kron_ref = bf16[1024,1024]{1,0:T(8,128)(2,1)} reshape(bf16[64,16,64,16]{3,2,1,0:T(8,128)(2,1)} %broadcast_multiply_fusion) | data formatting | bytes 4194304 | tf_op jit(solution)/shard_map/mul | solution.py:196
  100.9 0.7 constant_dynamic-slice_fusion.yback_ref
  101.6 1.8 reduce.1
  103.4 0.4 reshape.67
  103.8 1.1 copy.29
  105.0 3.0 %copy.31.spec_ref = f32[64,32,64]{2,1,0:T(8,128)} copy(f32[64,32,64]{0,2,1:T(8,128)} %bitcast.50) | data formatting | bytes 1048576 | tf_op jit(solution)/shard_map/reshape | solution.py:175
  107.9 89.9 %shard_map.139 = (bf16[64,256,512]{2,1,0:T(8,128)(2,1)}, f32[64,32,64]{2,1,0:T(8,128)}) custom-call(bf16[64,256,512]{2,1,0:T(8,128)(2,1)} %bitcast.42, bf16[64,256,512]{2,1,0:T(8,128)(2,1)} %bitcast.43, f32[64,32,64]{2,1,0:T(8,128)} %copy.31.spec_ref, f32[64,1,64]{2,1,0:T(1,128)} %pad.4.bias_ref, bf16[1024,1024]{1,0:T(8,128)(2,1)} %mul.79.kron_ref, ...), custom_call_target="tpu_custom_call" | custom-call | tf_op jit(solution)/shard_map/pallas_call | solution.py:142
  197.9 1.8 copy.32
  199.6 1.8 copy.33
  201.4 1.9 reshape.68
  203.3 21.5 %all_to_all.15 = f32[32,1,4096]{2,1,0:T(1,128)S(1)} all-to-all(f32[32,1,4096]{2,1,0:T(1,128)S(1)} %reshape.68), channel_id=1, replica_groups=mesh['dp'=16,'slab'=2] {'dp','slab'}, dimensions={0} | all-to-all | bytes 1048576 | tf_op jit(solution)/shard_map/all_to_all | solution.py:164
  224.8 1.8 reduce.2
  226.6 0.4 reshape.69
  227.0 1.0 reduce_sum.19
  228.0 0.3 fusion.10
  228.4 5.8 %divide_subtract_fusion = (f32[16,2,64,128]{3,2,1,0:T(8,128)}, f32[16,2,64,128]{3,2,1,0:T(8,128)}, f32[16,2,64,128]{3,2,1,0:T(8,128)}) fusion(f32[16,2,64,128]{3,2,1,0:T(8,128)S(1)} %copy-done, f32[16,2,64,128]{3,2,1,0:T(8,128)} %param.14, f32[16,2,64,128]{3,2,1,0:T(8,128)} %param.15, f32[16,2,16,1,64]{4,2,3,1,0:T(8,128)S(1)} %get-tuple-element.12, ...), kind=kOutput, calls=%fused_computation.6 | convolution fusion | flops 104136704 | bytes 7077888 | tf_op jit(solution)/shard_map/kjbri,kjbro->kjio/dot_general | solution.py:213
  (17 shorter events, 0.9 us)
Async XLA Ops:
  0.6 38.6 %copy-start.2 = (bf16[64,64]{1,0:T(8,128)(2,1)S(1)}, bf16[64,64]{1,0:T(8,128)(2,1)}, u32[]{:S(2)}) copy-start(bf16[64,64]{1,0:T(8,128)(2,1)} %param.16) | copy-start | bytes 24580
  0.6 38.7 %copy-start.3 = (f32[64]{0:T(128)S(1)}, f32[64]{0:T(128)}, u32[]{:S(2)}) copy-start(f32[64]{0:T(128)} %param.17) | copy-start | bytes 772
  0.7 58.2 %copy-start = (f32[16,2,64,128]{3,2,1,0:T(8,128)S(1)}, f32[16,2,64,128]{3,2,1,0:T(8,128)}, u32[]{:S(2)}) copy-start(f32[16,2,64,128]{3,2,1,0:T(8,128)} %param.13) | copy-start | bytes 3145732
  32.2 22.9 %all-to-all-start = ((f32[32,1,4096]{2,1,0:T(1,128)}), f32[32,1,4096]{2,1,0:T(1,128)S(1)}, u32[]{:S(2)}, u32[]{:S(2)}) async-start(f32[32,1,4096]{2,1,0:T(1,128)} %reshape.64), calls=%async_computation | async-start | bytes 1048576 | tf_op jit(solution)/shard_map/all_to_all | solution.py:164
  62.2 39.4 %all-to-all-start.1 = ((f32[32,1,4096]{2,1,0:T(1,128)}), f32[32,1,4096]{2,1,0:T(1,128)S(1)}, u32[]{:S(2)}, u32[]{:S(2)}) async-start(f32[32,1,4096]{2,1,0:T(1,128)} %reshape.66), calls=%async_computation.1 | async-start | bytes 1048576 | tf_op jit(solution)/shard_map/all_to_all | solution.py:173
  65.1 35.9 %copy-start.1 = (bf16[512,192]{1,0:T(8,128)(2,1)S(1)}, bf16[512,192]{1,0:T(8,128)(2,1)}, u32[]{:S(2)}) copy-start(bf16[512,192]{1,0:T(8,128)(2,1)} %constant.46.clone) | copy-start | bytes 589828

commit v2 on v1

--- a/solution.py
+++ b/solution.py
@@ -15,6 +15,7 @@
 KY = 32
 KZ = 32
 ROWS = 16
+SUB = 8
 
 high = lax.Precision.HIGHEST
 gelu_coef = 0.7978845608028654
@@ -48,24 +49,42 @@
     return jnp.dot(a, b, preferred_element_type=jnp.float32)
 
 
+def one_hot(shape, test):
+    rows = lax.broadcasted_iota(jnp.int32, shape, 0)
+    columns = lax.broadcasted_iota(jnp.int32, shape, 1)
+    return jnp.where(test(rows, columns), 1.0, 0.0).astype(jnp.bfloat16)
+
+
+def each(count, step):
+    per = 8
+
+    @pl.loop(0, count // per)
+    def _(i):
+        for n in range(per):
+            step(i * per + n)
+
+
 def y_modes(zval, ytab):
     top, rest = split(zval)
-    both = mm(ytab, top)
-    w = both[: 2 * KY] + both[2 * KY :] + mm(ytab[: 2 * KY], rest)
+    both = mm(ytab, jnp.concatenate([top, rest], axis=1))
+    first = both[: 2 * KY]
+    w = first[:, : 2 * KZ] + first[:, 2 * KZ :] + both[2 * KY :, : 2 * KZ]
     real = w[:KY, :KZ] + w[KY:, KZ:]
     imag = w[:KY, KZ:] - w[KY:, :KZ]
     return jnp.concatenate([real, imag], axis=1)
 
 
 def forward_kernel(x_ref, zt_ref, yt_ref, o_ref):
-    for c in range(x_ref.shape[0]):
-        zval = mm(x_ref[c], zt_ref[...])
-        o_ref[c] = y_modes(zval[:, : 2 * KZ] + zval[:, 2 * KZ :], yt_ref[...])
+    per, rows, length = x_ref.shape
+    zval = mm(x_ref[...].reshape(per * rows, length), zt_ref[...])
+    zval = (zval[:, : 2 * KZ] + zval[:, 2 * KZ :]).reshape(per, rows, 2 * KZ)
+    for c in range(per):
+        o_ref[c] = y_modes(zval[c], yt_ref[...])
 
 
 def point_kernel(
-    x_ref, cot_ref, spec_ref, bias_ref, kron_ref, zt_ref, yt_ref, back_ref, yback_ref,
-    out_ref, g_ref, left, zsum,
+    x_ref, cot_ref, spec_ref, bias_ref, skip_ref, zt_ref, yt_ref, back_ref, yback_ref,
+    out_ref, g_ref, left, zsum, kron_ref,
 ):
     step = pl.program_id(0)
     chans, rows = left.shape[:2]
@@ -73,8 +92,18 @@
 
     @pl.when(step == 0)
     def _():
-        @pl.loop(0, chans)
-        def _(o):
+        tall = chans * SUB
+        part = tall // 4
+        spread = one_hot((chans, tall), lambda i, r: i == r // SUB)
+        for m in range(4):
+            pick = one_hot((part, chans), lambda r, o: (r + m * part) // SUB == o)
+            rows_of = mm(pick, skip_ref[...]).astype(jnp.bfloat16)
+            same = one_hot((part, tall), lambda r, s: r % SUB == s % SUB)
+            kron_ref[m * part : (m + 1) * part, :] = (
+                mm(rows_of, spread).astype(jnp.bfloat16) * same
+            )
+
+        def invert(o):
             v = spec_ref[o]
             turned = jnp.concatenate([-v[:, KZ:], v[:, :KZ]], axis=1)
             top, rest = split(jnp.concatenate([v, turned], axis=0))
@@ -88,31 +117,38 @@
             terms = jnp.broadcast_to(terms, (rows, wide)).astype(jnp.bfloat16)
             left[o] = jnp.concatenate([ytop, yrest, ytop, terms], axis=1)
 
+        each(chans, invert)
+
     here = pl.ds(pl.multiple_of(step * ROWS, ROWS), ROWS)
-    x = x_ref[...].reshape(chans * ROWS, NZ)
-    part = chans // 2
-    for m in range(2):
-        own = slice(m * part, (m + 1) * part)
-        pre = mm(kron_ref[m * part * ROWS : (m + 1) * part * ROWS, :], x)
-        pre += mm(left[own, here, :].reshape(part * ROWS, 4 * wide), back_ref[...])
+    field = x_ref[...].astype(jnp.float32)
+    terms = left[:, here, :].astype(jnp.float32)
+    values = []
+    for m in range(ROWS // SUB):
+        own = slice(m * SUB, (m + 1) * SUB)
+        x = field[:, own].reshape(chans * SUB, NZ).astype(jnp.bfloat16)
+        term = terms[:, own].reshape(chans * SUB, 4 * wide).astype(jnp.bfloat16)
+        pre = mm(kron_ref[...], x) + mm(term, back_ref[...])
         sq = pre * pre
         t = jnp.tanh(pre * (gelu_coef + (gelu_coef * cube_coef) * sq))
         h = 0.5 + 0.5 * t
         value = pre * h
-        out_ref[own] = value.astype(jnp.bfloat16).reshape(part, ROWS, NZ)
+        values.append(value.reshape(chans, SUB, NZ))
         grow = 2.0 * gelu_coef + (6.0 * gelu_coef * cube_coef) * sq
-        cot = cot_ref[own].reshape(part * ROWS, NZ).astype(jnp.float32)
+        cot = cot_ref[...].astype(jnp.float32)[:, own].reshape(chans * SUB, NZ)
         slope = cot * (h + value * (0.5 - 0.5 * t) * grow)
         top, rest = split(slope)
         zval = mm(top, zt_ref[...])
         zval = zval[:, :wide] + zval[:, wide:] + mm(rest, zt_ref[:, :wide])
-        zsum[own, here, :] = zval.reshape(part, ROWS, wide)
+        place = pl.ds(pl.multiple_of(step * ROWS + m * SUB, SUB), SUB)
+        zsum[:, place, :] = zval.reshape(chans, SUB, wide)
+    out_ref[...] = jnp.concatenate(values, axis=1).astype(jnp.bfloat16)
 
     @pl.when(step == pl.num_programs(0) - 1)
     def _():
-        @pl.loop(0, chans)
-        def _(o):
+        def forward(o):
             g_ref[o] = y_modes(zsum[o], yt_ref[...])
+
+        each(chans, forward)
 
 
 def whole(shape):
@@ -136,14 +172,14 @@
     )(field, zt, yt)
 
 
-def point_part(field, cot, spec, bias, kron, zt, yt, back, yback):
+def point_part(field, cot, spec, bias, skip, zt, yt, back, yback):
     chans, rows, length = field.shape
     rowed = pl.BlockSpec((chans, ROWS, length), lambda i: (0, i, 0))
     return pl.pallas_call(
         point_kernel,
         grid=(rows // ROWS,),
         in_specs=[rowed, rowed]
-        + [whole(a.shape) for a in (spec, bias, kron, zt, yt, back, yback)],
+        + [whole(a.shape) for a in (spec, bias, skip, zt, yt, back, yback)],
         out_specs=[rowed, whole((chans, KY, 2 * KZ))],
         out_shape=[
             jax.ShapeDtypeStruct(field.shape, jnp.bfloat16),
@@ -152,9 +188,10 @@
         scratch_shapes=[
             pltpu.VMEM((chans, rows, 8 * KZ), jnp.bfloat16),
             pltpu.VMEM((chans, rows, 2 * KZ), jnp.float32),
+            pltpu.VMEM((chans * SUB, chans * SUB), jnp.bfloat16),
         ],
         compiler_params=pltpu.CompilerParams(vmem_limit_bytes=vmem_bytes),
-    )(field, cot, spec, bias, kron, zt, yt, back, yback)
+    )(field, cot, spec, bias, skip, zt, yt, back, yback)
 
 
 def to_owner(modes, dp, slab):
@@ -192,9 +229,6 @@
     yt = lax.dynamic_slice_in_dim(yt, start, rows, 1)
     yback = jnp.asarray(np.concatenate([ytop, ytop, yrest], 1))
     yback = lax.dynamic_slice_in_dim(yback, start, rows, 0)
-    same = jnp.eye(ROWS, dtype=jnp.bfloat16)
-    kron = w_skip.T[:, None, :, None] * same[None, :, None, :]
-    kron = kron.reshape(chans * ROWS, chans * ROWS)
     bias_lanes = jnp.pad(
         jnp.broadcast_to(bias[:, None, None], (chans, 1, 3)), ((0, 0), (0, 0), (0, 2 * KZ - 3))
     )
@@ -205,7 +239,7 @@
     vimag = prod[..., 0, chans:] + prod[..., 1, :chans]
     spec = from_owner(jnp.stack([vreal, vimag], 3) * out_scale, dp, slab)
     layer_out, gmodes = point_part(
-        snapshots[0], cotangent[0], spec, bias_lanes, kron, zt, yt, back, yback
+        snapshots[0], cotangent[0], spec, bias_lanes, w_skip.T, zt, yt, back, yback
     )
     g = to_owner(gmodes, dp, slab) * (out_scale / dp)
     turned = jnp.stack([g[..., 1, :], -g[..., 0, :]], 3)

time: 235 us -> 163 us (0.69)
  Pallas kernels: 114 us -> 68.1 us
  local copies, waits for them, and re-layouts: 52.1 us -> 20 us
  blocking collectives: 21.5 us -> 41.1 us
  starting transfers between devices: 9.9 us -> 2.81 us
  other arithmetic: 14.2 us -> 8.5 us
    pallas_call x1, Pallas kernels: 89.9 us -> 53.3 us  [point_part(): pl.pallas_call(point_kernel, grid=(rows // ROWS,), in_specs=[rowed, rowed...]
    mul x1 -> x0, local copies, waits for them, and re-layouts: 29.8 us -> none  [body(): kron = w_skip.T[:, None, :, None] * same[None, :, None, :]]
    all_to_all x1 -> x2, blocking collectives: 21.5 us -> 41.1 us  [to_owner(): lax.all_to_all(x, ('dp', 'slab'), split_axis=0, concat_axis=0, tiled=True)]
    all_to_all x1 -> x0, waiting for transfers between devices: 14.9 us -> none  [to_owner(): lax.all_to_all(x, ('dp', 'slab'), split_axis=0, concat_axis=0, tiled=True)]
    all_to_all x1, waiting for transfers between devices: 0.01 us -> 13.7 us  [from_owner(): lax.all_to_all(x, ('dp', 'slab'), split_axis=0, concat_axis=0, tiled=True)]
    pallas_call x1, Pallas kernels: 23.7 us -> 14.9 us  [forward_modes(): pl.pallas_call(forward_kernel, grid=(chans // per,), in_specs=[pl.BlockSp...]
    all_to_all x1 -> x0, starting transfers between devices: 7.09 us -> none  [to_owner(): lax.all_to_all(x, ('dp', 'slab'), split_axis=0, concat_axis=0, tiled=True)]
    mul x1 -> x0, other arithmetic: 6.11 us -> none  [body(): kron = w_skip.T[:, None, :, None] * same[None, :, None, :]]
  transfers between devices with their start and end apart: 2 -> 1, of which waited for: 1 -> 1; matrix products, arithmetic and copies ran while one was open for 16% -> 1% of each run, Pallas kernels for 0% -> 0%
where the time goes in v2:
time: 163 us; the launch traced here: 162 us
  Pallas kernels  68.1 us (42%)
  blocking collectives  41.1 us (25%)
  local copies, waits for them, and re-layouts  20 us (12%)
  waiting for transfers between devices  13.7 us (8%)
  other arithmetic  8.5 us (5%)
  matrix products  7.18 us (4%)
  starting transfers between devices  2.81 us (2%)
    pallas_call x1, Pallas kernels, point_part(): pl.pallas_call(point_kernel, grid=(rows // ROWS,), in_specs=[rowed, rowed...  53.3 us
    all_to_all x2, blocking collectives, to_owner(): lax.all_to_all(x, ('dp', 'slab'), split_axis=0, concat_axis=0, tiled=True)  41.1 us
    pallas_call x1, Pallas kernels, forward_modes(): pl.pallas_call(forward_kernel, grid=(chans // per,), in_specs=[pl.BlockSp...  14.9 us
    all_to_all x1, waiting for transfers between devices, from_owner(): lax.all_to_all(x, ('dp', 'slab'), split_axis=0, concat_axis=0, tiled=True)  13.7 us
    unnamed x15, local copies, waits for them, and re-layouts  5.91 us
    dot_general x1, matrix products, body(): grad = jnp.einsum('kjbri,kjbro->kjio', u, pair, precision=high)  5.84 us
    all_to_all x2, other arithmetic, to_owner(): lax.all_to_all(x, ('dp', 'slab'), split_axis=0, concat_axis=0, tiled=True)  3.87 us
  transfers between devices with their start and end apart: 1, of which 1 were waited for; matrix products, arithmetic and copies ran while one was open for 1% of the time, Pallas kernels for 0%

profile of v2, /device:TPU:1, one launch (start us, length us, event | category | flops | bytes accessed | tf_op | source)
XLA Modules:
  0.0 162.3 jit_solution(5828625482882387108)
XLA Ops:
  0.6 1.6 constant_dynamic-slice_fusion.1.yt_ref
  2.2 14.9 %shard_map.138 = f32[64,32,64]{2,1,0:T(8,128)} custom-call(bf16[64,256,512]{2,1,0:T(8,128)(2,1)} %bitcast.39, bf16[512,128]{1,0:T(8,128)(2,1)} %constant.43.clone.zt_ref, bf16[128,256]{1,0:T(8,128)(2,1)} %constant_dynamic-slice_fusion.1.yt_ref), custom_call_target="tpu_custom_call" | custom-call | tf_op jit(solution)/shard_map/pallas_call | solution.py:161
  17.1 1.8 %copy.25 = f32[64,32,64]{0,2,1:T(8,128)S(1)} copy(f32[64,32,64]{2,1,0:T(8,128)} %shard_map.138) | data formatting | bytes 1048576 | tf_op jit(solution)/shard_map/pallas_call | solution.py:161
  18.8 0.8 copy.26
  19.7 0.7 reshape.51
  20.3 22.7 %all_to_all.15 = f32[32,1,4096]{2,1,0:T(1,128)S(1)} all-to-all(f32[32,1,4096]{2,1,0:T(1,128)S(1)} %reshape.51), channel_id=1, replica_groups=mesh['dp'=16,'slab'=2] {'dp','slab'}, dimensions={0} | all-to-all | bytes 1048576 | tf_op jit(solution)/shard_map/all_to_all | solution.py:201
  43.0 0.6 broadcast.25
  43.6 1.9 %reduce = f32[32,4096]{1,0:T(8,128)S(1)} reduce(f32[32,1,4096]{2,1,0:T(1,128)S(1)} %all_to_all.15, f32[]{:T(128)} %broadcast.25), dimensions={1}, to_apply=%all_to_all.9.reduce_sub_computation | reduce | bytes 1048580 | tf_op jit(solution)/shard_map/all_to_all | solution.py:201
  45.6 0.4 reshape.52
  46.0 1.0 reduce_sum.18
  47.0 1.3 fusion.1
  48.4 0.2 slice_subtract_fusion
  49.0 1.4 reshape.53
  50.4 2.8 %all-to-all-start.1 = ((f32[32,1,4096]{2,1,0:T(1,128)}), f32[32,1,4096]{2,1,0:T(1,128)S(1)}, u32[]{:S(2)}, u32[]{:S(2)}) async-start(f32[32,1,4096]{2,1,0:T(1,128)} %reshape.53), calls=%async_computation.1 | async-start | bytes 1048576 | tf_op jit(solution)/shard_map/all_to_all | solution.py:210
  53.2 0.7 copy.30
  54.1 0.6 pad.4.bias_ref
  54.7 0.7 constant_dynamic-slice_fusion.yback_ref
  55.4 13.7 %all-to-all-done.1 = f32[32,1,4096]{2,1,0:T(1,128)S(1)} async-done(((f32[32,1,4096]{2,1,0:T(1,128)}), f32[32,1,4096]{2,1,0:T(1,128)S(1)}, u32[]{:S(2)}, u32[]{:S(2)}) %all-to-all-start.1) | async-done | bytes 524320 | tf_op jit(solution)/shard_map/all_to_all | solution.py:210
  69.0 1.9 %reduce.1 = f32[32,4096]{1,0:T(8,128)S(1)} reduce(f32[32,1,4096]{2,1,0:T(1,128)S(1)} %all-to-all-done.1, f32[]{:T(128)} %broadcast.25), dimensions={1}, to_apply=%all_to_all.10.reduce_sub_computation | reduce | bytes 1048580 | tf_op jit(solution)/shard_map/all_to_all | solution.py:210
  71.0 0.4 reshape.54
  71.4 1.1 copy.29
  72.5 3.0 %copy.31.spec_ref = f32[64,32,64]{2,1,0:T(8,128)} copy(f32[64,32,64]{0,2,1:T(8,128)} %bitcast.48) | data formatting | bytes 1048576 | tf_op jit(solution)/shard_map/reshape | solution.py:212
  75.5 53.3 %shard_map.139 = (bf16[64,256,512]{2,1,0:T(8,128)(2,1)}, f32[64,32,64]{2,1,0:T(8,128)}) custom-call(bf16[64,256,512]{2,1,0:T(8,128)(2,1)} %bitcast.40, bf16[64,256,512]{2,1,0:T(8,128)(2,1)} %bitcast.41, f32[64,32,64]{2,1,0:T(8,128)} %copy.31.spec_ref, f32[64,1,64]{2,1,0:T(1,128)} %pad.4.bias_ref, bf16[64,64]{1,0:T(8,128)(2,1)} %bitcast.52, ...), custom_call_target="tpu_custom_call" | custom-call | tf_op jit(solution)/shard_map/pallas_call | solution.py:178
  128.8 1.8 %copy.32 = f32[64,32,64]{0,2,1:T(8,128)S(1)} copy(f32[64,32,64]{2,1,0:T(8,128)} %get-tuple-element.7) | data formatting | bytes 1048576 | tf_op jit(solution)/shard_map/pallas_call | solution.py:178
  130.5 1.8 %copy.33 = f32[16,2,16,2,2,64]{5,4,3,2,1,0:T(2,128)} copy(f32[16,2,16,2,2,64]{5,2,1,4,3,0:T(8,128)S(1)} %bitcast.49) | data formatting | bytes 1048576 | tf_op jit(solution)/shard_map/transpose | solution.py:200
  132.3 1.9 %reshape.55 = f32[32,1,4096]{2,1,0:T(1,128)S(1)} reshape(f32[32,64,64]{2,1,0:T(8,128)} %bitcast.50) | data formatting | bytes 1048576
  134.2 18.4 %all_to_all.16 = f32[32,1,4096]{2,1,0:T(1,128)S(1)} all-to-all(f32[32,1,4096]{2,1,0:T(1,128)S(1)} %reshape.55), channel_id=1, replica_groups=mesh['dp'=16,'slab'=2] {'dp','slab'}, dimensions={0} | all-to-all | bytes 1048576 | tf_op jit(solution)/shard_map/all_to_all | solution.py:201
  152.6 1.9 %reduce.2 = f32[32,4096]{1,0:T(8,128)S(1)} reduce(f32[32,1,4096]{2,1,0:T(1,128)S(1)} %all_to_all.16, f32[]{:T(128)} %broadcast.25), dimensions={1}, to_apply=%all_to_all.11.reduce_sub_computation | reduce | bytes 1048580 | tf_op jit(solution)/shard_map/all_to_all | solution.py:201
  154.6 0.4 reshape.56
  155.0 1.0 reduce_sum.19
  156.0 0.3 fusion.10
  156.4 5.8 %divide_subtract_fusion = (f32[16,2,64,128]{3,2,1,0:T(8,128)}, f32[16,2,64,128]{3,2,1,0:T(8,128)}, f32[16,2,64,128]{3,2,1,0:T(8,128)}) fusion(f32[16,2,64,128]{3,2,1,0:T(8,128)S(1)} %copy-done, f32[16,2,64,128]{3,2,1,0:T(8,128)} %param.14, f32[16,2,64,128]{3,2,1,0:T(8,128)} %param.15, f32[16,2,16,1,64]{4,2,3,1,0:T(8,128)S(1)} %get-tuple-element.12, ...), kind=kOutput, calls=%fused_computation.5 | convolution fusion | flops 104136704 | bytes 7077888 | tf_op jit(solution)/shard_map/kjbri,kjbro->kjio/dot_general | solution.py:247
  (13 shorter events, 0.5 us)
Async XLA Ops:
  0.6 46.4 %copy-start = (f32[16,2,64,128]{3,2,1,0:T(8,128)S(1)}, f32[16,2,64,128]{3,2,1,0:T(8,128)}, u32[]{:S(2)}) copy-start(f32[16,2,64,128]{3,2,1,0:T(8,128)} %param.13) | copy-start | bytes 3145732
  2.2 51.0 %copy-start.2 = (bf16[64,64]{1,0:T(8,128)(2,1)S(1)}, bf16[64,64]{1,0:T(8,128)(2,1)}, u32[]{:S(2)}) copy-start(bf16[64,64]{1,0:T(8,128)(2,1)} %param.16) | copy-start | bytes 24580
  2.2 51.7 %copy-start.3 = (f32[64]{0:T(128)S(1)}, f32[64]{0:T(128)}, u32[]{:S(2)}) copy-start(f32[64]{0:T(128)} %param.17) | copy-start | bytes 772
  2.2 52.5 %copy-start.1 = (bf16[512,192]{1,0:T(8,128)(2,1)S(1)}, bf16[512,192]{1,0:T(8,128)(2,1)}, u32[]{:S(2)}) copy-start(bf16[512,192]{1,0:T(8,128)(2,1)} %constant.46.clone) | copy-start | bytes 589828
  50.4 18.6 %all-to-all-start.1 = ((f32[32,1,4096]{2,1,0:T(1,128)}), f32[32,1,4096]{2,1,0:T(1,128)S(1)}, u32[]{:S(2)}, u32[]{:S(2)}) async-start(f32[32,1,4096]{2,1,0:T(1,128)} %reshape.53), calls=%async_computation.1 | async-start | bytes 1048576 | tf_op jit(solution)/shard_map/all_to_all | solution.py:210
